TPU v7x, 32 devices: a whole 2x2x4 slice. The times are simulated.
32 devices in a mesh: grp: 2 (over y), wide: 8 (over z, x), tm: 2 (over core).
Axes of the slice: x: 2, y: 2, z: 4, core: 2. Of those that a mesh axis runs over, the one named last changes fastest.
Arguments:
- voltages: bfloat16 [2048, 65536], P('wide', ('grp', 'tm')), parts along dimension 1, may hold values from -6 to 6
- channels: int32 [16], replicated, may hold values from 0 to 1023, as said below
- tile_pairs: int32 [128, 2], replicated, may hold values from 0 to 31, as said below
Outputs:
- visibility: bfloat16 [32, 128, 64, 128], P(('grp', 'wide', 'tm')), parts along dimension 0
There are 2 independent parts, one for each index of `grp`. A program takes and returns all parts, laid end to end along the dimension named above; an argument that names none is the same for every part. Nothing has to cross between parts.
Inputs may be any that keep to these rules, and one draw needn't show every extreme that they name: `channels`: 16 different channel numbers in no fixed order; 0 and 1023 are always among them. `tile_pairs`: 128 different ordered tile pairs; (0, 0) and (31, 31) are always among them.
All inputs are finite; a program needn't handle non-finite values.
Results may differ from a plain program's by a relative error of at most 0.0071.
Values may be sent and summed in bfloat16 or wider, within the bound.
No kernel may reach another device: no remote copies, remote signals or barrier semaphores. Data moves between devices by JAX's collectives and lax.ppermute only.
A program may use at most 64 MiB of HBM per device.

v0:
```python
import jax
import jax.numpy as jnp
from jax import lax
from jax.sharding import PartitionSpec as P

TILE = 64
NFFT = 2048


def dft_table(channels, length):
    samples = jnp.arange(length, dtype=jnp.int32)
    phase = channels[:, None] * samples[None, :] % length
    angle = 2.0 * jnp.pi / length * phase.astype(jnp.float32)
    window = 0.5 - 0.5 * jnp.cos(2.0 * jnp.pi / length * samples.astype(jnp.float32))
    scale = 1.0 / jnp.sqrt(jnp.float32(0.375 * length))
    table = jnp.concatenate([window * jnp.cos(angle), -window * jnp.sin(angle)], 0) * scale
    return table.astype(jnp.bfloat16)


def corner_turn(spectrum):
    return lax.all_to_all(
        lax.all_to_all(spectrum, "wide", split_axis=1, concat_axis=2, tiled=True),
        "tm",
        split_axis=1,
        concat_axis=3,
        tiled=True,
    )


def shards(voltages, channels, tile_pairs):
    n_wide = lax.axis_size("wide")
    n_time = lax.axis_size("tm")
    in_dev = voltages.shape[0]
    frames_dev = voltages.shape[1] // NFFT
    count = channels.shape[0]
    per_dev = count // (n_wide * n_time)
    npairs = tile_pairs.shape[0]
    table = dft_table(channels, NFFT)

    def spectrum(start, frames):
        block = voltages.reshape(in_dev * frames, NFFT)
        result = lax.dot_general(
            table, block, (((1,), (1,)), ((), ())), preferred_element_type=jnp.float32
        )
        return result.astype(jnp.bfloat16).reshape(2, count, in_dev, frames)

    turned = corner_turn(spectrum(0, frames_dev))
    frames = turned.shape[3]
    tiles_all = turned.shape[2] // TILE
    tiled = turned.reshape(2, per_dev, tiles_all, TILE, frames)

    def stacked(which):
        picked = jnp.take(tiled, tile_pairs[:, which], axis=2)
        return picked.transpose(2, 1, 0, 3, 4).reshape(npairs, per_dev, 2 * TILE, frames)

    first = stacked(0)
    second = stacked(1)
    sums = jnp.einsum("pcif,pcjf->pcij", first, second, preferred_element_type=jnp.float32)
    frames_all = frames_dev * n_time
    real = sums[:, :, :TILE, :TILE] + sums[:, :, TILE:, TILE:]
    imag = sums[:, :, :TILE, TILE:] - sums[:, :, TILE:, :TILE]
    visibility = (jnp.concatenate([real, imag], 3) / frames_all).astype(jnp.bfloat16)
    return visibility.transpose(1, 0, 2, 3)


def solution(mesh):
    return jax.shard_map(
        shards,
        mesh=mesh,
        in_specs=(P("wide", ("grp", "tm")), P(), P()),
        out_specs=P(("grp", "wide", "tm"), None, None, None),
        check_vma=False,
    )
```

profile of v0, /device:TPU:0, one launch (start us, length us, event | category | flops | bytes accessed | tf_op | source)
XLA Modules:
  0.0 67.3 jit_solution(2652461978201646500)
XLA Ops:
  0.0 0.1 multiply_subtract_fusion
  0.1 13.5 %reshape.88 = bf16[2048,2048]{1,0:T(8,128)(2,1)} reshape(bf16[256,16384]{1,0:T(8,128)(2,1)} %param.5) | data formatting | bytes 16777216 | tf_op jit(solution)/shard_map/reshape | solution.py:41
  13.6 0.6 cosine_multiply_fusion
  14.2 0.0 copy-start
  14.2 6.0 %convolution_convert_fusion = bf16[32,2048]{1,0:T(8,128)(2,1)S(1)} fusion(bf16[2048,2048]{1,0:T(8,128)(2,1)} %reshape.88, f32[16,2048]{1,0:T(8,128)S(1)} %get-tuple-element.15, f32[16,2048]{1,0:T(8,128)S(1)} %get-tuple-element.14), kind=kOutput, calls=%fused_computation.9 | convolution fusion | flops 268697600 | bytes 8781824 | tf_op jit(solution)/shard_map/dot_general | solution.py:42
  20.2 0.3 copy.21
  20.5 0.4 reshape.89
  20.9 1.6 %copy.22 = bf16[2,16,256,8]{2,3,0,1:T(8,128)(2,1)} copy(bf16[2,16,256,8]{1,0,3,2:T(2,128)(2,1)S(1)} %reshape.89) | data formatting | bytes 262144 | tf_op jit(solution)/shard_map/reshape | solution.py:45
  22.5 7.3 %all-to-all-start = ((bf16[2,16,256,8]{2,3,0,1:T(8,128)(2,1)}), bf16[2,16,256,8]{2,3,0,1:T(8,128)(2,1)S(1)}, u32[]{:S(2)}, u32[]{:S(2)}) async-start(bf16[2,16,256,8]{2,3,0,1:T(8,128)(2,1)} %copy.22), calls=%async_computation | async-start | bytes 262144 | tf_op jit(solution)/shard_map/all_to_all | solution.py:22
  29.8 7.3 %all-to-all-done = bf16[2,16,256,8]{2,3,0,1:T(8,128)(2,1)S(1)} async-done(((bf16[2,16,256,8]{2,3,0,1:T(8,128)(2,1)}), bf16[2,16,256,8]{2,3,0,1:T(8,128)(2,1)S(1)}, u32[]{:S(2)}, u32[]{:S(2)}) %all-to-all-start) | async-done | bytes 131104 | tf_op jit(solution)/shard_map/all_to_all | solution.py:22
  37.1 3.8 %all_to_all.33 = bf16[2,2,2048,8]{2,3,0,1:T(8,128)(2,1)S(1)} all-to-all(bf16[2,2,2048,8]{2,3,0,1:T(8,128)(2,1)S(1)} %copy.25), channel_id=1, replica_groups=mesh['grp'=2,'wide'=8,'tm'=2] {'tm'}, dimensions={1} | all-to-all | bytes 262144 | tf_op jit(solution)/shard_map/all_to_all | solution.py:21
  41.0 0.2 reshape.90
  41.2 0.1 copy.35
  41.3 0.8 %gather_fusion.1 = bf16[128,2,64,16]{2,3,1,0:T(8,128)(2,1)S(1)} fusion(bf16[2,32,64,16]{2,3,1,0:T(8,128)(2,1)S(1)} %bitcast.50, s32[1024]{0:T(1024)S(1)} %get-tuple-element.18), kind=kCustom, calls=%fused_computation.1.clone | custom fusion | bytes 1049088 | tf_op jit(solution)/shard_map/jit(_take)/gather | solution.py:53
  42.1 0.2 fusion.3
  42.4 1.4 %copy.30 = bf16[128,1,2,64,16]{0,4,3,2,1:T(8,128)(2,1)S(1)} copy(bf16[128,1,2,64,16]{3,4,2,0,1:T(8,128)(2,1)S(1)} %fusion.3) | data formatting | bytes 1048576 | tf_op jit(solution)/shard_map/transpose | solution.py:54
  43.8 0.7 %copy.32 = bf16[128,128,16]{1,2,0:T(8,128)(2,1)S(1)} copy(bf16[128,128,16]{0,2,1:T(8,128)(2,1)S(1)} %bitcast.52) | data formatting | bytes 1048576 | tf_op jit(solution)/shard_map/reshape.3
  44.5 0.8 %gather_fusion = bf16[128,2,64,16]{2,3,1,0:T(8,128)(2,1)S(1)} fusion(bf16[2,32,64,16]{2,3,1,0:T(8,128)(2,1)S(1)} %bitcast.51, s32[1024]{0:T(1024)S(1)} %get-tuple-element.19), kind=kCustom, calls=%fused_computation.clone | custom fusion | bytes 1049088 | tf_op jit(solution)/shard_map/jit(_take)/gather | solution.py:53
  45.3 0.2 fusion.4
  45.5 1.4 %copy.28 = bf16[128,1,2,64,16]{0,4,3,2,1:T(8,128)(2,1)S(1)} copy(bf16[128,1,2,64,16]{3,4,2,0,1:T(8,128)(2,1)S(1)} %fusion.4) | data formatting | bytes 1048576 | tf_op jit(solution)/shard_map/transpose | solution.py:54
  46.9 0.7 %copy.31 = bf16[128,128,16]{1,2,0:T(8,128)(2,1)S(1)} copy(bf16[128,128,16]{0,2,1:T(8,128)(2,1)S(1)} %bitcast.53) | data formatting | bytes 1048576 | tf_op jit(solution)/shard_map/reshape.2
  47.7 4.5 %convolution_bitcast_fusion = f32[128,1,128,128]{3,2,0,1:T(8,128)} fusion(bf16[128,128,16]{1,2,0:T(8,128)(2,1)S(1)} %copy.31, bf16[128,128,16]{1,2,0:T(8,128)(2,1)S(1)} %copy.32), kind=kOutput, calls=%fused_computation.8 | convolution fusion | flops 67108864 | bytes 9437184 | tf_op jit(solution)/shard_map/pcif,pcjf->pcij/dot_general | solution.py:58
  52.2 10.4 %fusion.1 = (f32[1,128,64,64]{3,2,1,0:T(8,128)S(1)}, f32[1,128,64,64]{3,2,1,0:T(8,128)}) fusion(f32[128,1,128,128]{3,2,0,1:T(8,128)} %convolution_bitcast_fusion), kind=kLoop, calls=%fused_computation.5 | loop fusion | flops 1048576 | bytes 12582912 | tf_op jit(solution)/shard_map/concatenate | solution.py:62
  62.6 4.7 %fusion.2 = bf16[1,128,64,128]{3,2,1,0:T(8,128)(2,1)} fusion(f32[1,128,64,64]{3,2,1,0:T(8,128)} %get-tuple-element.11, f32[1,128,64,64]{3,2,1,0:T(8,128)S(1)} %get-tuple-element.10), kind=kLoop, calls=%fused_computation.7 | loop fusion | flops 3145728 | bytes 6291456 | tf_op jit(solution)/shard_map/convert_element_type | solution.py:62
  (8 shorter events, 0.1 us)
Async XLA Ops:
  0.1 13.5 %copy-start.1 = (s32[16]{0:T(128)S(1)}, s32[16]{0:T(128)}, u32[]{:S(2)}) copy-start(s32[16]{0:T(128)} %param.6) | copy-start | bytes 196
  14.2 15.5 %copy-start = (s32[128,2]{0,1:T(2,128)S(1)}, s32[128,2]{0,1:T(2,128)}, u32[]{:S(2)}) copy-start(s32[128,2]{0,1:T(2,128)} %param.7) | copy-start | bytes 3076
  22.5 14.6 %all-to-all-start = ((bf16[2,16,256,8]{2,3,0,1:T(8,128)(2,1)}), bf16[2,16,256,8]{2,3,0,1:T(8,128)(2,1)S(1)}, u32[]{:S(2)}, u32[]{:S(2)}) async-start(bf16[2,16,256,8]{2,3,0,1:T(8,128)(2,1)} %copy.22), calls=%async_computation | async-start | bytes 262144 | tf_op jit(solution)/shard_map/all_to_all | solution.py:22
where the time goes:
time: 67.9 us; the launch traced here: 67.3 us
  local copies, waits for them, and re-layouts  22.1 us (33%)
  other arithmetic  16.1 us (24%)
  matrix products  10.5 us (15%)
  waiting for transfers between devices  7.31 us (11%)
  starting transfers between devices  7.25 us (11%)
  blocking collectives  3.84 us (6%)
    reshape x1, local copies, waits for them, and re-layouts, spectrum(): block = voltages.reshape(in_dev * frames, NFFT)  13.5 us
    concatenate x1, other arithmetic, shards(): jnp.concatenate([real, imag], 3) / frames_all  10.4 us
    all_to_all x1, waiting for transfers between devices, corner_turn(): lax.all_to_all(spectrum, 'wide', split_axis=1, concat_axis=2, tiled=True)  7.31 us
    all_to_all x1, starting transfers between devices, corner_turn(): lax.all_to_all(spectrum, 'wide', split_axis=1, concat_axis=2, tiled=True)  7.25 us
    dot_general x1, matrix products, spectrum(): lax.dot_general(table, block, (((1,), (1,)), ((), ())), preferred_element...  5.97 us
    convert_element_type x1, other arithmetic, shards(): (jnp.concatenate([real, imag], 3) / frames_all).astype(jnp.bfloat16)  4.66 us
    dot_general x1, matrix products, shards(): jnp.einsum('pcif,pcjf->pcij', first, second, preferred_element_type=jnp.f...  4.53 us
    all_to_all x1, blocking collectives, corner_turn(): lax.all_to_all(lax.all_to_all(spectrum, 'wide', split_axis=1, concat_axis...  3.84 us
  transfers between devices with their start and end apart: 1, of which 1 were waited for; matrix products, arithmetic and copies ran while one was open for 0% of the time, Pallas kernels for 0%

commit v1 on v0

v1 whole, which is shorter than its diff:
```python
import functools
import math

import jax
import jax.numpy as jnp
from jax import lax
from jax.experimental import pallas as pl
from jax.experimental.pallas import tpu as pltpu
from jax.sharding import PartitionSpec as P

TILE = 64
NFFT = 2048
LANES = 128
VMEM_LIMIT = 48 * 1024 * 1024


def cos_sin(phase):
    quarter = NFFT // 4
    turn = (phase + quarter // 2) // quarter
    x = (phase - turn * quarter).astype(jnp.float32) * (2.0 * math.pi / NFFT)
    y = x * x
    c = 1.0 + y * (-1 / 2 + y * (1 / 24 + y * (-1 / 720 + y * (1 / 40320))))
    s = x * (1.0 + y * (-1 / 6 + y * (1 / 120 + y * (-1 / 5040 + y * (1 / 362880)))))
    odd = (turn & 1) == 1
    cos = jnp.where(odd, s, c)
    sin = jnp.where(odd, c, s)
    cos = jnp.where(((turn + 1) & 2) == 2, -cos, cos)
    sin = jnp.where((turn & 2) == 2, -sin, sin)
    return cos, sin


def fill_table(chan_ref, table):
    count = table.shape[0] // 2
    rows = lax.broadcasted_iota(jnp.int32, (count, LANES), 0)
    chan = jnp.zeros((count, LANES), jnp.int32)
    for s in range(count):
        chan = jnp.where(rows == s, chan_ref[s], chan)
    lane = lax.broadcasted_iota(jnp.int32, (count, LANES), 1)
    scale = 1.0 / math.sqrt(0.375 * NFFT)
    for start in range(0, NFFT, LANES):
        n = lane + start
        window = 0.5 - 0.5 * cos_sin(n[:8])[0]
        window = jnp.tile(window * scale, (count // 8, 1))
        cos, sin = cos_sin((chan * n) & (NFFT - 1))
        table[:count, start : start + LANES] = (window * cos).astype(table.dtype)
        table[count:, start : start + LANES] = (-window * sin).astype(table.dtype)


def spectra_kernel(chan_hbm, volt_hbm, out_ref, chan, volt, table, spec, chan_sem, sems):
    frames = volt.shape[0]
    count = spec.shape[0]
    chan_copy = pltpu.make_async_copy(chan_hbm, chan, chan_sem)
    chan_copy.start()
    copies = []
    for f in range(frames):
        copy = pltpu.make_async_copy(
            volt_hbm.at[:, f * NFFT : (f + 1) * NFFT], volt.at[f], sems.at[f]
        )
        copy.start()
        copies.append(copy)
    chan_copy.wait()
    fill_table(chan, table)
    for f in range(frames):
        copies[f].wait()
        result = lax.dot_general(
            table[...], volt[f], (((1,), (1,)), ((), ())), preferred_element_type=jnp.float32
        )
        spec[:, f, :] = result[:count]
        spec[:, frames + f, :] = result[count:]
    out_ref[...] = spec[...].astype(out_ref.dtype)


def spectra_of(voltages, channels):
    in_dev = voltages.shape[0]
    frames = voltages.shape[1] // NFFT
    count = channels.shape[0]
    return pl.pallas_call(
        spectra_kernel,
        out_shape=jax.ShapeDtypeStruct((count, 2 * frames, in_dev), jnp.bfloat16),
        in_specs=[pl.BlockSpec(memory_space=pl.ANY)] * 2,
        out_specs=pl.BlockSpec(memory_space=pltpu.VMEM),
        scratch_shapes=[
            pltpu.SMEM((count,), jnp.int32),
            pltpu.VMEM((frames, in_dev, NFFT), voltages.dtype),
            pltpu.VMEM((2 * count, NFFT), jnp.bfloat16),
            pltpu.VMEM((count, 2 * frames, in_dev), jnp.float32),
            pltpu.SemaphoreType.DMA,
            pltpu.SemaphoreType.DMA((frames,)),
        ],
        compiler_params=pltpu.CompilerParams(vmem_limit_bytes=VMEM_LIMIT),
        name="spectra",
    )(channels, voltages)


def pairs_kernel(scale, pairs_ref, turned_ref, out_hbm, left, right, out, sems):
    blocks, times, rows, width = turned_ref.shape
    half = rows // 2
    depth = times * rows
    low = lax.broadcasted_iota(jnp.int32, (rows, LANES), 1) < TILE
    per_lane = LANES // TILE
    for w in range(blocks):
        stacks = []
        for t in range(times):
            x = turned_ref[w, t].astype(jnp.float32)
            stacks.append(x)
            m = jnp.concatenate([x[half:], -x[:half]], 0)
            for c in range(width // LANES):
                xc = x[:, c * LANES : (c + 1) * LANES]
                mc = m[:, c * LANES : (c + 1) * LANES]
                tile = w * (width // TILE) + c * per_lane
                even = jnp.where(low, xc, pltpu.roll(mc, TILE, 1))
                odd = jnp.where(low, pltpu.roll(xc, TILE, 1), mc)
                right[tile, t * rows : (t + 1) * rows] = even.astype(right.dtype)
                right[tile + 1, t * rows : (t + 1) * rows] = odd.astype(right.dtype)
        stack = jnp.concatenate(stacks, 0)
        for u in range(width // LANES):
            turned = stack[:, u * LANES : (u + 1) * LANES].T.astype(left.dtype)
            tile = w * (width // TILE) + u * per_lane
            left[tile] = turned[:TILE]
            left[tile + 1] = turned[TILE:]

    npairs = out.shape[0]
    parts = sems.shape[0]
    step = npairs // parts
    copies = []
    for part in range(parts):

        @pl.loop(0, step, unroll=8)
        def _(i):
            p = part * step + i
            prod = lax.dot_general(
                left[pairs_ref[2 * p]],
                right[pairs_ref[2 * p + 1]],
                (((1,), (0,)), ((), ())),
                preferred_element_type=jnp.float32,
            )
            out[p] = (prod * scale).astype(out.dtype)

        span = pl.ds(part * step, step)
        copy = pltpu.make_async_copy(out.at[span], out_hbm.at[span], sems.at[part])
        copy.start()
        copies.append(copy)
    for copy in copies:
        copy.wait()


def products_of(turned, tile_pairs, frames_all):
    blocks, times, rows, width = turned.shape
    npairs = tile_pairs.shape[0]
    tiles = blocks * width // TILE
    depth = times * rows
    return pl.pallas_call(
        functools.partial(pairs_kernel, 1.0 / frames_all),
        out_shape=jax.ShapeDtypeStruct((npairs, TILE, 2 * TILE), jnp.bfloat16),
        in_specs=[
            pl.BlockSpec(memory_space=pltpu.SMEM),
            pl.BlockSpec(memory_space=pltpu.VMEM),
        ],
        out_specs=pl.BlockSpec(memory_space=pl.ANY),
        scratch_shapes=[
            pltpu.VMEM((tiles, TILE, depth), jnp.bfloat16),
            pltpu.VMEM((tiles, depth, 2 * TILE), jnp.bfloat16),
            pltpu.VMEM((npairs, TILE, 2 * TILE), jnp.bfloat16),
            pltpu.SemaphoreType.DMA((4,)),
        ],
        compiler_params=pltpu.CompilerParams(vmem_limit_bytes=VMEM_LIMIT),
        name="pair_products",
    )(tile_pairs.reshape(-1), turned)


def shards(voltages, channels, tile_pairs):
    n_wide = lax.axis_size("wide")
    n_time = lax.axis_size("tm")
    in_dev = voltages.shape[0]
    frames_dev = voltages.shape[1] // NFFT
    count = channels.shape[0]
    per_dev = count // (n_wide * n_time)
    rows = 2 * frames_dev

    spectra = spectra_of(voltages, channels)
    turned = lax.all_to_all(spectra, ("wide", "tm"), split_axis=0, concat_axis=0, tiled=True)
    turned = turned.reshape(n_wide, n_time, per_dev, rows, in_dev)
    results = []
    for c in range(per_dev):
        one = turned[:, :, c]
        if in_dev % LANES:
            one = one.transpose(1, 2, 0, 3).reshape(1, n_time, rows, n_wide * in_dev)
        results.append(products_of(one, tile_pairs, frames_dev * n_time))
    return jnp.stack(results)


def solution(mesh):
    return jax.shard_map(
        shards,
        mesh=mesh,
        in_specs=(P("wide", ("grp", "tm")), P(), P()),
        out_specs=P(("grp", "wide", "tm"), None, None, None),
        check_vma=False,
    )
```

time: 67.9 us -> 27.9 us (0.41)
  local copies, waits for them, and re-layouts: 22.1 us -> 0.91 us
  other arithmetic: 16.1 us -> 0 us
  Pallas kernels: 0 us -> 11.7 us
  matrix products: 10.5 us -> 0 us
  blocking collectives: 3.84 us -> 0 us
    reshape x5 -> x1, local copies, waits for them, and re-layouts: 15.9 us -> 0.14 us  [products_of(): tile_pairs.reshape(-1)]
    pallas_call x0 -> x2, Pallas kernels: none -> 11.7 us  [the longest x1 7.37 us: spectra_of(): pl.pallas_call(spectra_kernel, out_shape=jax.ShapeDtypeStruct((count, 2 *...]
    dot_general x2 -> x0, matrix products: 10.5 us -> none  [the longest x1 5.97 us: spectrum(): lax.dot_general(table, block, (((1,), (1,)), ((), ())), preferred_element...]
    concatenate x1 -> x0, other arithmetic: 10.4 us -> none  [shards(): jnp.concatenate([real, imag], 3) / frames_all]
    convert_element_type x1 -> x0, other arithmetic: 4.66 us -> none  [shards(): (jnp.concatenate([real, imag], 3) / frames_all).astype(jnp.bfloat16)]
    all_to_all x1 -> x0, blocking collectives: 3.84 us -> none  [corner_turn(): lax.all_to_all(lax.all_to_all(spectrum, 'wide', split_axis=1, concat_axis...]
    transpose x2 -> x0, local copies, waits for them, and re-layouts: 2.78 us -> none  [stacked(): picked.transpose(2, 1, 0, 3, 4).reshape(npairs, per_dev, 2 * TILE, frames)]
    gather x2 -> x0, local copies, waits for them, and re-layouts: 1.64 us -> none  [stacked(): picked = jnp.take(tiled, tile_pairs[:, which], axis=2)]
  transfers between devices with their start and end apart: 1 -> 1, of which waited for: 1 -> 1; matrix products, arithmetic and copies ran while one was open for 0% -> 1% of each run, Pallas kernels for 0% -> 0%
where the time goes in v1:
time: 27.9 us; the launch traced here: 27.7 us
  Pallas kernels  11.7 us (42%)
  waiting for transfers between devices  7.67 us (27%)
  starting transfers between devices  7.37 us (26%)
  local copies, waits for them, and re-layouts  0.91 us (3%)
    all_to_all x1, waiting for transfers between devices, shards(): lax.all_to_all(spectra, ('wide', 'tm'), split_axis=0, concat_axis=0, tile...  7.67 us
    all_to_all x1, starting transfers between devices, shards(): lax.all_to_all(spectra, ('wide', 'tm'), split_axis=0, concat_axis=0, tile...  7.37 us
    pallas_call x1, Pallas kernels, spectra_of(): pl.pallas_call(spectra_kernel, out_shape=jax.ShapeDtypeStruct((count, 2 *...  7.37 us
    pallas_call x1, Pallas kernels, products_of(): pl.pallas_call(functools.partial(pairs_kernel, 1.0 / frames_all), out_sha...  4.33 us
    unnamed x5, local copies, waits for them, and re-layouts  0.77 us
  transfers between devices with their start and end apart: 1, of which 1 were waited for; matrix products, arithmetic and copies ran while one was open for 1% of the time, Pallas kernels for 0%

profile of v1, /device:TPU:0, one launch (start us, length us, event | category | flops | bytes accessed | tf_op | source)
XLA Modules:
  0.0 27.7 jit_solution(9442922516842625281)
XLA Ops:
  0.0 0.0 copy-start
  0.0 0.7 %copy-done = s32[16]{0:T(128)S(1)} copy-done((s32[16]{0:T(128)S(1)}, s32[16]{0:T(128)}, u32[]{:S(2)}) %copy-start) | copy-done | bytes 88
  0.7 0.0 copy-start.1
  0.7 7.4 %spectra.1 = bf16[16,16,256]{2,1,0:T(8,128)(2,1)} custom-call(s32[16]{0:T(128)S(1)} %copy-done, bf16[256,16384]{1,0:T(8,128)(2,1)} %volt_hbm.1), custom_call_target="tpu_custom_call" | custom-call | tf_op jit(solution)/shard_map/spectra/pallas_call | solution.py:77
  8.0 7.4 %all-to-all-start = ((bf16[16,16,256]{2,1,0:T(8,128)(2,1)}), bf16[16,16,256]{2,1,0:T(8,128)(2,1)S(1)}, u32[]{:S(2)}, u32[]{:S(2)}) async-start(bf16[16,16,256]{2,1,0:T(8,128)(2,1)} %spectra.1), calls=%async_computation | async-start | bytes 262144 | tf_op jit(solution)/shard_map/all_to_all | solution.py:181
  15.4 0.0 copy-done.1
  15.4 0.1 copy.4
  15.5 0.1 reshape.3.pairs_ref
  15.7 7.7 %all-to-all-done = bf16[16,16,256]{2,1,0:T(8,128)(2,1)S(1)} async-done(((bf16[16,16,256]{2,1,0:T(8,128)(2,1)}), bf16[16,16,256]{2,1,0:T(8,128)(2,1)S(1)}, u32[]{:S(2)}, u32[]{:S(2)}) %all-to-all-start) | async-done | bytes 131104 | tf_op jit(solution)/shard_map/all_to_all | solution.py:181
  23.3 4.3 %pair_products.1 = bf16[128,64,128]{2,1,0:T(8,128)(2,1)} custom-call(s32[256]{0:T(256)S(1)} %reshape.3.pairs_ref, bf16[8,2,16,256]{3,2,1,0:T(8,128)(2,1)S(1)} %bitcast.2), custom_call_target="tpu_custom_call" | custom-call | tf_op jit(solution)/shard_map/pair_products/pallas_call | solution.py:152
Async XLA Ops:
  0.0 0.7 %copy-start = (s32[16]{0:T(128)S(1)}, s32[16]{0:T(128)}, u32[]{:S(2)}) copy-start(s32[16]{0:T(128)} %chan_hbm.1) | copy-start | bytes 196
  0.7 14.8 %copy-start.1 = (s32[128,2]{0,1:T(2,128)S(1)}, s32[128,2]{0,1:T(2,128)}, u32[]{:S(2)}) copy-start(s32[128,2]{0,1:T(2,128)} %param.5) | copy-start | bytes 3076
  8.0 15.3 %all-to-all-start = ((bf16[16,16,256]{2,1,0:T(8,128)(2,1)}), bf16[16,16,256]{2,1,0:T(8,128)(2,1)S(1)}, u32[]{:S(2)}, u32[]{:S(2)}) async-start(bf16[16,16,256]{2,1,0:T(8,128)(2,1)} %spectra.1), calls=%async_computation | async-start | bytes 262144 | tf_op jit(solution)/shard_map/all_to_all | solution.py:181

commit v2 on v1

v2 whole, which is shorter than its diff:
```python
import functools
import math

import jax
import jax.numpy as jnp
from jax import lax
from jax.experimental import pallas as pl
from jax.experimental.pallas import tpu as pltpu
from jax.sharding import PartitionSpec as P

TILE = 64
NFFT = 2048
LANES = 128
VMEM_LIMIT = 48 * 1024 * 1024


def divisor(n, most):
    return max(d for d in range(1, most + 1) if n % d == 0)


def cos_sin(phase):
    quarter = NFFT // 4
    turn = (phase + quarter // 2) // quarter
    x = (phase - turn * quarter).astype(jnp.float32) * (2.0 * math.pi / NFFT)
    y = x * x
    c = 1.0 + y * (-1 / 2 + y * (1 / 24 + y * (-1 / 720 + y * (1 / 40320))))
    s = x * (1.0 + y * (-1 / 6 + y * (1 / 120 + y * (-1 / 5040 + y * (1 / 362880)))))
    odd = (turn & 1) == 1
    cos = jnp.where(odd, s, c)
    sin = jnp.where(odd, c, s)
    cos = jnp.where(((turn + 1) & 2) == 2, -cos, cos)
    sin = jnp.where((turn & 2) == 2, -sin, sin)
    return cos, sin


def fill_table(order, chan_ref, table):
    count = table.shape[0] // 2
    rows = lax.broadcasted_iota(jnp.int32, (count, LANES), 0)
    chan = jnp.zeros((count, LANES), jnp.int32)
    for s in range(count):
        chan = jnp.where(rows == s, chan_ref[order[s]], chan)
    lane = lax.broadcasted_iota(jnp.int32, (count, LANES), 1)
    scale = 1.0 / math.sqrt(0.375 * NFFT)

    @pl.loop(0, NFFT // LANES)
    def _(j):
        start = pl.multiple_of(j * LANES, LANES)
        n = lane + start
        window = 0.5 - 0.5 * cos_sin(n[:8])[0]
        window = jnp.tile(window * scale, (count // 8, 1))
        cos, sin = cos_sin((chan * n) & (NFFT - 1))
        table[:count, pl.ds(start, LANES)] = (window * cos).astype(table.dtype)
        table[count:, pl.ds(start, LANES)] = (-window * sin).astype(table.dtype)


def spectra_kernel(order, chan_hbm, volt_hbm, out_ref, chan, volt, table, spec, chan_sem, sems):
    frames, in_dev = volt.shape[:2]
    count = spec.shape[0]

    def frame(f):
        start = pl.multiple_of(f * NFFT, NFFT)
        return pltpu.make_async_copy(volt_hbm.at[:, pl.ds(start, NFFT)], volt.at[f], sems.at[f])

    chan_copy = pltpu.make_async_copy(chan_hbm, chan, chan_sem)
    chan_copy.start()

    @pl.loop(0, frames)
    def _(f):
        frame(f).start()

    chan_copy.wait()
    fill_table(order, chan, table)

    @pl.loop(0, frames)
    def _(f):
        frame(f).wait()
        result = lax.dot_general(
            table[...], volt[f], (((1,), (1,)), ((), ())), preferred_element_type=jnp.float32
        )
        spec[:, pl.ds(f, 1), :] = result[:count].reshape(count, 1, in_dev)
        spec[:, pl.ds(frames + f, 1), :] = result[count:].reshape(count, 1, in_dev)

    out_ref[...] = spec[...].astype(out_ref.dtype)


def spectra_of(voltages, channels, order):
    in_dev = voltages.shape[0]
    frames = voltages.shape[1] // NFFT
    count = channels.shape[0]
    return pl.pallas_call(
        functools.partial(spectra_kernel, order),
        out_shape=jax.ShapeDtypeStruct((count, 2 * frames, in_dev), jnp.bfloat16),
        in_specs=[pl.BlockSpec(memory_space=pl.ANY)] * 2,
        out_specs=pl.BlockSpec(memory_space=pltpu.VMEM),
        scratch_shapes=[
            pltpu.SMEM((count,), jnp.int32),
            pltpu.VMEM((frames, in_dev, NFFT), voltages.dtype),
            pltpu.VMEM((2 * count, NFFT), jnp.bfloat16),
            pltpu.VMEM((count, 2 * frames, in_dev), jnp.float32),
            pltpu.SemaphoreType.DMA,
            pltpu.SemaphoreType.DMA((frames,)),
        ],
        compiler_params=pltpu.CompilerParams(vmem_limit_bytes=VMEM_LIMIT),
        name="spectra",
    )(pltpu.with_memory_space_constraint(channels, pltpu.HBM), voltages)


def pairs_kernel(scale, places, pairs_ref, turned_ref, out_hbm, left, right, out, sems):
    sources, rows, width = turned_ref.shape
    times = len(places[0])
    half = rows // 2
    low = lax.broadcasted_iota(jnp.int32, (rows, LANES), 1) < TILE
    for w, place in enumerate(places):
        stack = []
        for t in range(times):
            x = turned_ref[place[t]].astype(jnp.float32)
            stack.append(x)
            m = jnp.concatenate([x[half:], -x[:half]], 0)
            for u in range(width // LANES):
                xu = x[:, u * LANES : (u + 1) * LANES]
                mu = m[:, u * LANES : (u + 1) * LANES]
                tile = (w * width + u * LANES) // TILE
                depth = slice(t * rows, (t + 1) * rows)
                first = jnp.where(low, xu, pltpu.roll(mu, TILE, 1))
                second = jnp.where(low, pltpu.roll(xu, TILE, 1), mu)
                right[tile, depth] = first.astype(right.dtype)
                right[tile + 1, depth] = second.astype(right.dtype)
        stack = jnp.concatenate(stack, 0)
        for u in range(width // LANES):
            turned = stack[:, u * LANES : (u + 1) * LANES].T.astype(left.dtype)
            tile = (w * width + u * LANES) // TILE
            left[tile] = turned[:TILE]
            left[tile + 1] = turned[TILE:]

    parts = sems.shape[0]
    step = out.shape[0] // parts

    def part(i):
        span = pl.ds(i * step, step)
        return pltpu.make_async_copy(out.at[span], out_hbm.at[span], sems.at[i])

    @pl.loop(0, parts)
    def _(i):
        for k in range(step):
            p = i * step + k
            product = lax.dot_general(
                left[pairs_ref[2 * p]],
                right[pairs_ref[2 * p + 1]],
                (((1,), (0,)), ((), ())),
                preferred_element_type=jnp.float32,
            )
            out[p] = (product * scale).astype(out.dtype)
        part(i).start()

    @pl.loop(0, parts)
    def _(i):
        part(i).wait()


def products_of(turned, places, tile_pairs, frames_all):
    sources, rows, width = turned.shape
    npairs = tile_pairs.shape[0]
    depth = len(places[0]) * rows
    tiles = len(places) * width // TILE
    return pl.pallas_call(
        functools.partial(pairs_kernel, 1.0 / frames_all, places),
        out_shape=jax.ShapeDtypeStruct((npairs, TILE, 2 * TILE), jnp.bfloat16),
        in_specs=[
            pl.BlockSpec(memory_space=pltpu.SMEM),
            pl.BlockSpec(memory_space=pltpu.VMEM),
        ],
        out_specs=pl.BlockSpec(memory_space=pl.ANY),
        scratch_shapes=[
            pltpu.VMEM((tiles, TILE, depth), jnp.bfloat16),
            pltpu.VMEM((tiles, depth, 2 * TILE), jnp.bfloat16),
            pltpu.VMEM((npairs, TILE, 2 * TILE), jnp.bfloat16),
            pltpu.SemaphoreType.DMA((npairs // divisor(npairs, 32),)),
        ],
        compiler_params=pltpu.CompilerParams(vmem_limit_bytes=VMEM_LIMIT),
        name="pair_products",
    )(tile_pairs.reshape(-1), turned)


def shards(voltages, channels, tile_pairs):
    n_wide = lax.axis_size("wide")
    n_time = lax.axis_size("tm")
    n_dev = n_wide * n_time
    in_dev = voltages.shape[0]
    frames_dev = voltages.shape[1] // NFFT
    count = channels.shape[0]
    per_dev = count // n_dev
    rows = 2 * frames_dev

    middle = n_wide // 2 * n_time + n_time - 1
    group = [middle] + [d for d in range(n_dev) if d != middle]
    place = {d: j for j, d in enumerate(group)}
    order = [d * per_dev + c for d in group for c in range(per_dev)]

    spectra = spectra_of(voltages, channels, order)
    turned = lax.all_to_all(
        spectra, ("wide", "tm"), split_axis=0, concat_axis=0, axis_index_groups=[group], tiled=True
    )
    turned = turned.reshape(n_dev, per_dev, rows, in_dev)
    results = []
    for c in range(per_dev):
        one = turned[:, c]
        places = [[place[w * n_time + t] for t in range(n_time)] for w in range(n_wide)]
        if in_dev % LANES:
            one = jnp.concatenate([one[1 : middle + 1], one[:1], one[middle + 1 :]], 0)
            one = one.reshape(n_wide, n_time, rows, in_dev).transpose(1, 2, 0, 3)
            one = one.reshape(n_time, rows, n_wide * in_dev)
            places = [list(range(n_time))]
        results.append(products_of(one, places, tile_pairs, frames_dev * n_time))
    return jnp.stack(results)


def solution(mesh):
    return jax.shard_map(
        shards,
        mesh=mesh,
        in_specs=(P("wide", ("grp", "tm")), P(), P()),
        out_specs=P(("grp", "wide", "tm"), None, None, None),
        check_vma=False,
    )
```

time: 27.9 us -> 21.4 us (0.77)
  Pallas kernels: 11.7 us -> 8.35 us
  waiting for transfers between devices: 7.67 us -> 4.96 us
  local copies, waits for them, and re-layouts: 0.91 us -> 0.25 us
    pallas_call x2, Pallas kernels: 11.7 us -> 8.35 us  [the longest x1 5.57 us: spectra_of(): pl.pallas_call(functools.partial(spectra_kernel, order), out_shape=jax.Sh...]
    all_to_all x1, waiting for transfers between devices: 7.67 us -> 4.96 us  [shards(): lax.all_to_all(spectra, ('wide', 'tm'), split_axis=0, concat_axis=0, axis...]
    unnamed x5 -> x3, local copies, waits for them, and re-layouts: 0.77 us -> 0.12 us
where the time goes in v2:
time: 21.4 us; the launch traced here: 21.1 us
  Pallas kernels  8.35 us (39%)
  starting transfers between devices  7.56 us (35%)
  waiting for transfers between devices  4.96 us (23%)
  local copies, waits for them, and re-layouts  0.25 us (1%)
    all_to_all x1, starting transfers between devices, shards(): lax.all_to_all(spectra, ('wide', 'tm'), split_axis=0, concat_axis=0, axis...  7.56 us
    pallas_call x1, Pallas kernels, spectra_of(): pl.pallas_call(functools.partial(spectra_kernel, order), out_shape=jax.Sh...  5.57 us
    all_to_all x1, waiting for transfers between devices, shards(): lax.all_to_all(spectra, ('wide', 'tm'), split_axis=0, concat_axis=0, axis...  4.96 us
    pallas_call x1, Pallas kernels, products_of(): pl.pallas_call(functools.partial(pairs_kernel, 1.0 / frames_all, places),...  2.79 us
  transfers between devices with their start and end apart: 1, of which 1 were waited for; matrix products, arithmetic and copies ran while one was open for 1% of the time, Pallas kernels for 0%

profile of v2, /device:TPU:0, one launch (start us, length us, event | category | flops | bytes accessed | tf_op | source)
XLA Modules:
  0.0 21.1 jit_solution(8527839724085088768)
XLA Ops:
  0.0 0.0 copy-start
  0.0 5.6 %spectra.1 = bf16[16,16,256]{2,1,0:T(8,128)(2,1)} custom-call(s32[16]{0:T(128)} %chan_hbm.1, bf16[256,16384]{1,0:T(8,128)(2,1)} %volt_hbm.1), custom_call_target="tpu_custom_call" | custom-call | tf_op jit(solution)/shard_map/spectra/pallas_call | solution.py:90
  5.6 7.6 %all-to-all-start = ((bf16[16,16,256]{2,1,0:T(8,128)(2,1)}), bf16[16,16,256]{2,1,0:T(8,128)(2,1)S(1)}, u32[]{:S(2)}, u32[]{:S(2)}) async-start(bf16[16,16,256]{2,1,0:T(8,128)(2,1)} %spectra.1), calls=%async_computation | async-start | bytes 262144 | tf_op jit(solution)/shard_map/all_to_all | solution.py:200
  13.1 0.0 copy-done
  13.1 0.1 copy.4
  13.3 0.1 reshape.3.pairs_ref
  13.4 5.0 %all-to-all-done.turned_ref = bf16[16,16,256]{2,1,0:T(8,128)(2,1)S(1)} async-done(((bf16[16,16,256]{2,1,0:T(8,128)(2,1)}), bf16[16,16,256]{2,1,0:T(8,128)(2,1)S(1)}, u32[]{:S(2)}, u32[]{:S(2)}) %all-to-all-start) | async-done | bytes 131104 | tf_op jit(solution)/shard_map/all_to_all | solution.py:200
  18.4 2.8 %pair_products.1 = bf16[128,64,128]{2,1,0:T(8,128)(2,1)} custom-call(s32[256]{0:T(256)S(1)} %reshape.3.pairs_ref, bf16[16,16,256]{2,1,0:T(8,128)(2,1)S(1)} %all-to-all-done.turned_ref), custom_call_target="tpu_custom_call" | custom-call | tf_op jit(solution)/shard_map/pair_products/pallas_call | solution.py:165
Async XLA Ops:
  0.0 13.1 %copy-start = (s32[128,2]{0,1:T(2,128)S(1)}, s32[128,2]{0,1:T(2,128)}, u32[]{:S(2)}) copy-start(s32[128,2]{0,1:T(2,128)} %param.5) | copy-start | bytes 3076
  5.6 12.8 %all-to-all-start = ((bf16[16,16,256]{2,1,0:T(8,128)(2,1)}), bf16[16,16,256]{2,1,0:T(8,128)(2,1)S(1)}, u32[]{:S(2)}, u32[]{:S(2)}) async-start(bf16[16,16,256]{2,1,0:T(8,128)(2,1)} %spectra.1), calls=%async_computation | async-start | bytes 262144 | tf_op jit(solution)/shard_map/all_to_all | solution.py:200

commit v3 on v2

--- a/solution.py
+++ b/solution.py
@@ -181,6 +181,13 @@
     )(tile_pairs.reshape(-1), turned)
 
 
+def turn_group(n_wide, n_time):
+    middle = (n_wide // 2 + 1) * n_time - 1 + (n_time if n_wide > 2 else 0)
+    plane = 2 * n_time
+    others = [d for d in range(n_wide * n_time) if d != middle]
+    return [middle] + sorted(others, key=lambda d: (-abs(d // plane - middle // plane), d))
+
+
 def shards(voltages, channels, tile_pairs):
     n_wide = lax.axis_size("wide")
     n_time = lax.axis_size("tm")
@@ -191,8 +198,7 @@
     per_dev = count // n_dev
     rows = 2 * frames_dev
 
-    middle = n_wide // 2 * n_time + n_time - 1
-    group = [middle] + [d for d in range(n_dev) if d != middle]
+    group = turn_group(n_wide, n_time)
     place = {d: j for j, d in enumerate(group)}
     order = [d * per_dev + c for d in group for c in range(per_dev)]
 
@@ -206,7 +212,7 @@
         one = turned[:, c]
         places = [[place[w * n_time + t] for t in range(n_time)] for w in range(n_wide)]
         if in_dev % LANES:
-            one = jnp.concatenate([one[1 : middle + 1], one[:1], one[middle + 1 :]], 0)
+            one = jnp.take(one, jnp.array([place[d] for d in range(n_dev)]), axis=0)
             one = one.reshape(n_wide, n_time, rows, in_dev).transpose(1, 2, 0, 3)
             one = one.reshape(n_time, rows, n_wide * in_dev)
             places = [list(range(n_time))]

time: 21.4 us -> 20.3 us (0.949)
  waiting for transfers between devices: 4.96 us -> 3.56 us
    all_to_all x1, waiting for transfers between devices: 4.96 us -> 3.56 us  [shards(): lax.all_to_all(spectra, ('wide', 'tm'), split_axis=0, concat_axis=0, axis...]
where the time goes in v3:
time: 20.3 us; the launch traced here: 19.9 us
  Pallas kernels  8.36 us (41%)
  starting transfers between devices  7.72 us (38%)
  waiting for transfers between devices  3.56 us (18%)
  local copies, waits for them, and re-layouts  0.25 us (1%)
    all_to_all x1, starting transfers between devices, shards(): lax.all_to_all(spectra, ('wide', 'tm'), split_axis=0, concat_axis=0, axis...  7.72 us
    pallas_call x1, Pallas kernels, spectra_of(): pl.pallas_call(functools.partial(spectra_kernel, order), out_shape=jax.Sh...  5.57 us
    all_to_all x1, waiting for transfers between devices, shards(): lax.all_to_all(spectra, ('wide', 'tm'), split_axis=0, concat_axis=0, axis...  3.56 us
    pallas_call x1, Pallas kernels, products_of(): pl.pallas_call(functools.partial(pairs_kernel, 1.0 / frames_all, places),...  2.79 us
  transfers between devices with their start and end apart: 1, of which 1 were waited for; matrix products, arithmetic and copies ran while one was open for 1% of the time, Pallas kernels for 0%

profile of v3, /device:TPU:0, one launch (start us, length us, event | category | flops | bytes accessed | tf_op | source)
XLA Modules:
  0.0 19.9 jit_solution(4366938043822204984)
XLA Ops:
  0.0 0.0 copy-start
  0.0 5.6 %spectra.1 = bf16[16,16,256]{2,1,0:T(8,128)(2,1)} custom-call(s32[16]{0:T(128)} %chan_hbm.1, bf16[256,16384]{1,0:T(8,128)(2,1)} %volt_hbm.1), custom_call_target="tpu_custom_call" | custom-call | tf_op jit(solution)/shard_map/spectra/pallas_call | solution.py:90
  5.6 7.7 %all-to-all-start = ((bf16[16,16,256]{2,1,0:T(8,128)(2,1)}), bf16[16,16,256]{2,1,0:T(8,128)(2,1)S(1)}, u32[]{:S(2)}, u32[]{:S(2)}) async-start(bf16[16,16,256]{2,1,0:T(8,128)(2,1)} %spectra.1), calls=%async_computation | async-start | bytes 262144 | tf_op jit(solution)/shard_map/all_to_all | solution.py:206
  13.3 0.0 copy-done
  13.3 0.1 copy.4
  13.4 0.1 reshape.3.pairs_ref
  13.6 3.6 %all-to-all-done.turned_ref = bf16[16,16,256]{2,1,0:T(8,128)(2,1)S(1)} async-done(((bf16[16,16,256]{2,1,0:T(8,128)(2,1)}), bf16[16,16,256]{2,1,0:T(8,128)(2,1)S(1)}, u32[]{:S(2)}, u32[]{:S(2)}) %all-to-all-start) | async-done | bytes 131104 | tf_op jit(solution)/shard_map/all_to_all | solution.py:206
  17.1 2.8 %pair_products.1 = bf16[128,64,128]{2,1,0:T(8,128)(2,1)} custom-call(s32[256]{0:T(256)S(1)} %reshape.3.pairs_ref, bf16[16,16,256]{2,1,0:T(8,128)(2,1)S(1)} %all-to-all-done.turned_ref), custom_call_target="tpu_custom_call" | custom-call | tf_op jit(solution)/shard_map/pair_products/pallas_call | solution.py:165
Async XLA Ops:
  0.0 13.3 %copy-start = (s32[128,2]{0,1:T(2,128)S(1)}, s32[128,2]{0,1:T(2,128)}, u32[]{:S(2)}) copy-start(s32[128,2]{0,1:T(2,128)} %param.5) | copy-start | bytes 3076
  5.6 11.5 %all-to-all-start = ((bf16[16,16,256]{2,1,0:T(8,128)(2,1)}), bf16[16,16,256]{2,1,0:T(8,128)(2,1)S(1)}, u32[]{:S(2)}, u32[]{:S(2)}) async-start(bf16[16,16,256]{2,1,0:T(8,128)(2,1)} %spectra.1), calls=%async_computation | async-start | bytes 262144 | tf_op jit(solution)/shard_map/all_to_all | solution.py:206

commit v4 on v3

--- a/solution.py
+++ b/solution.py
@@ -71,14 +71,27 @@
     chan_copy.wait()
     fill_table(order, chan, table)
 
-    @pl.loop(0, frames)
+    def transform(f, several):
+        for k in range(several):
+            frame(f + k).wait()
+        block = volt[pl.ds(f, several)].reshape(several * in_dev, NFFT)
+        result = lax.dot_general(
+            table[...], block, (((1,), (1,)), ((), ())), preferred_element_type=jnp.float32
+        )
+        for k in range(several):
+            part = result[:, k * in_dev : (k + 1) * in_dev]
+            spec[:, pl.ds(f + k, 1), :] = part[:count].reshape(count, 1, in_dev)
+            spec[:, pl.ds(frames + f + k, 1), :] = part[count:].reshape(count, 1, in_dev)
+
+    singles = min(frames, 2 + frames % 2)
+
+    @pl.loop(0, singles)
     def _(f):
-        frame(f).wait()
-        result = lax.dot_general(
-            table[...], volt[f], (((1,), (1,)), ((), ())), preferred_element_type=jnp.float32
-        )
-        spec[:, pl.ds(f, 1), :] = result[:count].reshape(count, 1, in_dev)
-        spec[:, pl.ds(frames + f, 1), :] = result[count:].reshape(count, 1, in_dev)
+        transform(f, 1)
+
+    @pl.loop(0, (frames - singles) // 2)
+    def _(g):
+        transform(singles + 2 * g, 2)
 
     out_ref[...] = spec[...].astype(out_ref.dtype)
 
@@ -105,7 +118,11 @@
     )(pltpu.with_memory_space_constraint(channels, pltpu.HBM), voltages)
 
 
-def pairs_kernel(scale, places, pairs_ref, turned_ref, out_hbm, left, right, out, sems):
+def pairs_kernel(
+    scale, places, pairs_any, turned_ref, out_hbm, pairs_ref, left, right, out, pairs_sem, sems
+):
+    pairs_copy = pltpu.make_async_copy(pairs_any, pairs_ref, pairs_sem)
+    pairs_copy.start()
     sources, rows, width = turned_ref.shape
     times = len(places[0])
     half = rows // 2
@@ -134,15 +151,11 @@
 
     parts = sems.shape[0]
     step = out.shape[0] // parts
-
-    def part(i):
-        span = pl.ds(i * step, step)
-        return pltpu.make_async_copy(out.at[span], out_hbm.at[span], sems.at[i])
-
-    @pl.loop(0, parts)
-    def _(i):
-        for k in range(step):
-            p = i * step + k
+    pairs_copy.wait()
+    copies = []
+    for i in range(parts):
+        span = slice(i * step, (i + 1) * step)
+        for p in range(i * step, (i + 1) * step):
             product = lax.dot_general(
                 left[pairs_ref[2 * p]],
                 right[pairs_ref[2 * p + 1]],
@@ -150,11 +163,10 @@
                 preferred_element_type=jnp.float32,
             )
             out[p] = (product * scale).astype(out.dtype)
-        part(i).start()
-
-    @pl.loop(0, parts)
-    def _(i):
-        part(i).wait()
+        copies.append(pltpu.make_async_copy(out.at[span], out_hbm.at[span], sems.at[i]))
+        copies[-1].start()
+    for copy in copies:
+        copy.wait()
 
 
 def products_of(turned, places, tile_pairs, frames_all):
@@ -166,14 +178,16 @@
         functools.partial(pairs_kernel, 1.0 / frames_all, places),
         out_shape=jax.ShapeDtypeStruct((npairs, TILE, 2 * TILE), jnp.bfloat16),
         in_specs=[
-            pl.BlockSpec(memory_space=pltpu.SMEM),
+            pl.BlockSpec(memory_space=pl.ANY),
             pl.BlockSpec(memory_space=pltpu.VMEM),
         ],
         out_specs=pl.BlockSpec(memory_space=pl.ANY),
         scratch_shapes=[
+            pltpu.SMEM((2 * npairs,), jnp.int32),
             pltpu.VMEM((tiles, TILE, depth), jnp.bfloat16),
             pltpu.VMEM((tiles, depth, 2 * TILE), jnp.bfloat16),
             pltpu.VMEM((npairs, TILE, 2 * TILE), jnp.bfloat16),
+            pltpu.SemaphoreType.DMA,
             pltpu.SemaphoreType.DMA((npairs // divisor(npairs, 32),)),
         ],
         compiler_params=pltpu.CompilerParams(vmem_limit_bytes=VMEM_LIMIT),

time: 20.3 us -> 19.3 us (0.951)
  Pallas kernels: 8.36 us -> 7.41 us
    pallas_call x1, Pallas kernels: 2.79 us -> 2.18 us  [products_of(): pl.pallas_call(functools.partial(pairs_kernel, 1.0 / frames_all, places),...]
    pallas_call x1, Pallas kernels: 5.57 us -> 5.22 us  [spectra_of(): pl.pallas_call(functools.partial(spectra_kernel, order), out_shape=jax.Sh...]
where the time goes in v4:
time: 19.3 us; the launch traced here: 19 us
  starting transfers between devices  7.71 us (40%)
  Pallas kernels  7.41 us (38%)
  waiting for transfers between devices  3.56 us (18%)
  local copies, waits for them, and re-layouts  0.25 us (1%)
    all_to_all x1, starting transfers between devices, shards(): lax.all_to_all(spectra, ('wide', 'tm'), split_axis=0, concat_axis=0, axis...  7.71 us
    pallas_call x1, Pallas kernels, spectra_of(): pl.pallas_call(functools.partial(spectra_kernel, order), out_shape=jax.Sh...  5.22 us
    all_to_all x1, waiting for transfers between devices, shards(): lax.all_to_all(spectra, ('wide', 'tm'), split_axis=0, concat_axis=0, axis...  3.56 us
    pallas_call x1, Pallas kernels, products_of(): pl.pallas_call(functools.partial(pairs_kernel, 1.0 / frames_all, places),...  2.18 us
  transfers between devices with their start and end apart: 1, of which 1 were waited for; matrix products, arithmetic and copies ran while one was open for 1% of the time, Pallas kernels for 0%

profile of v4, /device:TPU:0, one launch (start us, length us, event | category | flops | bytes accessed | tf_op | source)
XLA Modules:
  0.0 19.0 jit_solution(2439249099251048982)
XLA Ops:
  0.0 0.0 copy-start
  0.0 5.2 %spectra.1 = bf16[16,16,256]{2,1,0:T(8,128)(2,1)} custom-call(s32[16]{0:T(128)} %chan_hbm.1, bf16[256,16384]{1,0:T(8,128)(2,1)} %volt_hbm.1), custom_call_target="tpu_custom_call" | custom-call | tf_op jit(solution)/shard_map/spectra/pallas_call | solution.py:103
  5.2 7.7 %all-to-all-start = ((bf16[16,16,256]{2,1,0:T(8,128)(2,1)}), bf16[16,16,256]{2,1,0:T(8,128)(2,1)S(1)}, u32[]{:S(2)}, u32[]{:S(2)}) async-start(bf16[16,16,256]{2,1,0:T(8,128)(2,1)} %spectra.1), calls=%async_computation | async-start | bytes 262144 | tf_op jit(solution)/shard_map/all_to_all | solution.py:220
  12.9 0.0 copy-done
  13.0 0.1 copy.4
  13.1 0.1 reshape.3.pairs_any
  13.2 3.6 %all-to-all-done.turned_ref = bf16[16,16,256]{2,1,0:T(8,128)(2,1)S(1)} async-done(((bf16[16,16,256]{2,1,0:T(8,128)(2,1)}), bf16[16,16,256]{2,1,0:T(8,128)(2,1)S(1)}, u32[]{:S(2)}, u32[]{:S(2)}) %all-to-all-start) | async-done | bytes 131104 | tf_op jit(solution)/shard_map/all_to_all | solution.py:220
  16.8 2.2 %pair_products.1 = bf16[128,64,128]{2,1,0:T(8,128)(2,1)} custom-call(s32[256]{0:T(256)S(1)} %reshape.3.pairs_any, bf16[16,16,256]{2,1,0:T(8,128)(2,1)S(1)} %all-to-all-done.turned_ref), custom_call_target="tpu_custom_call" | custom-call | tf_op jit(solution)/shard_map/pair_products/pallas_call | solution.py:177
Async XLA Ops:
  0.0 12.9 %copy-start = (s32[128,2]{0,1:T(2,128)S(1)}, s32[128,2]{0,1:T(2,128)}, u32[]{:S(2)}) copy-start(s32[128,2]{0,1:T(2,128)} %param.5) | copy-start | bytes 3076
  5.2 11.5 %all-to-all-start = ((bf16[16,16,256]{2,1,0:T(8,128)(2,1)}), bf16[16,16,256]{2,1,0:T(8,128)(2,1)S(1)}, u32[]{:S(2)}, u32[]{:S(2)}) async-start(bf16[16,16,256]{2,1,0:T(8,128)(2,1)} %spectra.1), calls=%async_computation | async-start | bytes 262144 | tf_op jit(solution)/shard_map/all_to_all | solution.py:220

commit v5 on v4

--- a/solution.py
+++ b/solution.py
@@ -157,8 +157,8 @@
         span = slice(i * step, (i + 1) * step)
         for p in range(i * step, (i + 1) * step):
             product = lax.dot_general(
-                left[pairs_ref[2 * p]],
-                right[pairs_ref[2 * p + 1]],
+                left[pairs_ref[0, p]],
+                right[pairs_ref[1, p]],
                 (((1,), (0,)), ((), ())),
                 preferred_element_type=jnp.float32,
             )
@@ -183,7 +183,7 @@
         ],
         out_specs=pl.BlockSpec(memory_space=pl.ANY),
         scratch_shapes=[
-            pltpu.SMEM((2 * npairs,), jnp.int32),
+            pltpu.SMEM((2, npairs), jnp.int32),
             pltpu.VMEM((tiles, TILE, depth), jnp.bfloat16),
             pltpu.VMEM((tiles, depth, 2 * TILE), jnp.bfloat16),
             pltpu.VMEM((npairs, TILE, 2 * TILE), jnp.bfloat16),
@@ -192,7 +192,7 @@
         ],
         compiler_params=pltpu.CompilerParams(vmem_limit_bytes=VMEM_LIMIT),
         name="pair_products",
-    )(tile_pairs.reshape(-1), turned)
+    )(tile_pairs.T, turned)
 
 
 def turn_group(n_wide, n_time):

time: 19.3 us -> 18.2 us (0.943)
  blocking collectives: 0 us -> 11.1 us
  starting transfers between devices: 7.71 us -> 0 us
  waiting for transfers between devices: 3.56 us -> 0 us
  Pallas kernels: 7.41 us -> 6.75 us
  local copies, waits for them, and re-layouts: 0.25 us -> 0.01 us
    all_to_all x0 -> x1, blocking collectives: none -> 11.1 us  [shards(): lax.all_to_all(spectra, ('wide', 'tm'), split_axis=0, concat_axis=0, axis...]
    all_to_all x1 -> x0, starting transfers between devices: 7.71 us -> none  [shards(): lax.all_to_all(spectra, ('wide', 'tm'), split_axis=0, concat_axis=0, axis...]
    all_to_all x1 -> x0, waiting for transfers between devices: 3.56 us -> none  [shards(): lax.all_to_all(spectra, ('wide', 'tm'), split_axis=0, concat_axis=0, axis...]
    pallas_call x1, Pallas kernels: 5.22 us -> 4.57 us  [spectra_of(): pl.pallas_call(functools.partial(spectra_kernel, order), out_shape=jax.Sh...]
  transfers between devices with their start and end apart: 1 -> 0, of which waited for: 1 -> 0; matrix products, arithmetic and copies ran while one was open for 1% -> 0% of each run, Pallas kernels for 0% -> 0%
where the time goes in v5:
time: 18.2 us; the launch traced here: 17.9 us
  blocking collectives  11.1 us (61%)
  Pallas kernels  6.75 us (37%)
    all_to_all x1, blocking collectives, shards(): lax.all_to_all(spectra, ('wide', 'tm'), split_axis=0, concat_axis=0, axis...  11.1 us
    pallas_call x1, Pallas kernels, spectra_of(): pl.pallas_call(functools.partial(spectra_kernel, order), out_shape=jax.Sh...  4.57 us
    pallas_call x1, Pallas kernels, products_of(): pl.pallas_call(functools.partial(pairs_kernel, 1.0 / frames_all, places),...  2.18 us

profile of v5, /device:TPU:0, one launch (start us, length us, event | category | flops | bytes accessed | tf_op | source)
XLA Modules:
  0.0 17.9 jit_solution(2577135783487752507)
XLA Ops:
  0.0 0.0 copy-start
  0.0 4.6 %spectra.1 = bf16[16,16,256]{2,1,0:T(8,128)(2,1)S(1)} custom-call(s32[16]{0:T(128)} %chan_hbm.1, bf16[256,16384]{1,0:T(8,128)(2,1)} %volt_hbm.1), custom_call_target="tpu_custom_call" | custom-call | tf_op jit(solution)/shard_map/spectra/pallas_call | solution.py:103
  4.6 11.1 %all_to_all.5.turned_ref = bf16[16,16,256]{2,1,0:T(8,128)(2,1)S(1)} all-to-all(bf16[16,16,256]{2,1,0:T(8,128)(2,1)S(1)} %spectra.1), channel_id=1, replica_groups={{11,0,1,2,3,4,5,6,7,12,13,14,15,8,9,10},{27,16,17,18,19,20,21,22,23,28,..., dimensions={0} | all-to-all | bytes 262144 | tf_op jit(solution)/shard_map/all_to_all | solution.py:220
  15.7 0.0 copy-done
  15.7 2.2 %pair_products.1 = bf16[128,64,128]{2,1,0:T(8,128)(2,1)} custom-call(s32[2,128]{1,0:T(2,128)S(1)} %bitcast.2, bf16[16,16,256]{2,1,0:T(8,128)(2,1)S(1)} %all_to_all.5.turned_ref), custom_call_target="tpu_custom_call" | custom-call | tf_op jit(solution)/shard_map/pair_products/pallas_call | solution.py:177
Async XLA Ops:
  0.0 15.7 %copy-start = (s32[128,2]{0,1:T(2,128)S(1)}, s32[128,2]{0,1:T(2,128)}, u32[]{:S(2)}) copy-start(s32[128,2]{0,1:T(2,128)} %param.5) | copy-start | bytes 3076

commit v6 on v5

--- a/solution.py
+++ b/solution.py
@@ -53,7 +53,9 @@
         table[count:, pl.ds(start, LANES)] = (-window * sin).astype(table.dtype)
 
 
-def spectra_kernel(order, chan_hbm, volt_hbm, out_ref, chan, volt, table, spec, chan_sem, sems):
+def spectra_kernel(
+    order, chan_hbm, pairs_hbm, volt_hbm, out_ref, pairs_ref, chan, volt, table, spec, list_sems, sems
+):
     frames, in_dev = volt.shape[:2]
     count = spec.shape[0]
 
@@ -61,14 +63,17 @@
         start = pl.multiple_of(f * NFFT, NFFT)
         return pltpu.make_async_copy(volt_hbm.at[:, pl.ds(start, NFFT)], volt.at[f], sems.at[f])
 
-    chan_copy = pltpu.make_async_copy(chan_hbm, chan, chan_sem)
+    chan_copy = pltpu.make_async_copy(chan_hbm, chan, list_sems.at[0])
     chan_copy.start()
+    pairs_copy = pltpu.make_async_copy(pairs_hbm, pairs_ref, list_sems.at[1])
+    pairs_copy.start()
 
     @pl.loop(0, frames)
     def _(f):
         frame(f).start()
 
     chan_copy.wait()
+    pairs_copy.wait()
     fill_table(order, chan, table)
 
     def transform(f, several):
@@ -96,33 +101,36 @@
     out_ref[...] = spec[...].astype(out_ref.dtype)
 
 
-def spectra_of(voltages, channels, order):
+def spectra_of(voltages, channels, tile_pairs, order):
     in_dev = voltages.shape[0]
     frames = voltages.shape[1] // NFFT
     count = channels.shape[0]
+    lists = [pltpu.with_memory_space_constraint(x, pltpu.HBM) for x in (channels, tile_pairs.T)]
     return pl.pallas_call(
         functools.partial(spectra_kernel, order),
-        out_shape=jax.ShapeDtypeStruct((count, 2 * frames, in_dev), jnp.bfloat16),
-        in_specs=[pl.BlockSpec(memory_space=pl.ANY)] * 2,
-        out_specs=pl.BlockSpec(memory_space=pltpu.VMEM),
+        out_shape=(
+            jax.ShapeDtypeStruct((count, 2 * frames, in_dev), jnp.bfloat16),
+            pltpu.SMEM(lists[1].shape, jnp.int32),
+        ),
+        in_specs=[pl.BlockSpec(memory_space=pl.ANY)] * 3,
+        out_specs=(
+            pl.BlockSpec(memory_space=pltpu.VMEM),
+            pl.BlockSpec(memory_space=pltpu.SMEM),
+        ),
         scratch_shapes=[
             pltpu.SMEM((count,), jnp.int32),
             pltpu.VMEM((frames, in_dev, NFFT), voltages.dtype),
             pltpu.VMEM((2 * count, NFFT), jnp.bfloat16),
             pltpu.VMEM((count, 2 * frames, in_dev), jnp.float32),
-            pltpu.SemaphoreType.DMA,
+            pltpu.SemaphoreType.DMA((2,)),
             pltpu.SemaphoreType.DMA((frames,)),
         ],
         compiler_params=pltpu.CompilerParams(vmem_limit_bytes=VMEM_LIMIT),
         name="spectra",
-    )(pltpu.with_memory_space_constraint(channels, pltpu.HBM), voltages)
-
-
-def pairs_kernel(
-    scale, places, pairs_any, turned_ref, out_hbm, pairs_ref, left, right, out, pairs_sem, sems
-):
-    pairs_copy = pltpu.make_async_copy(pairs_any, pairs_ref, pairs_sem)
-    pairs_copy.start()
+    )(*lists, voltages)
+
+
+def pairs_kernel(scale, places, pairs_ref, turned_ref, out_hbm, left, right, out, sems):
     sources, rows, width = turned_ref.shape
     times = len(places[0])
     half = rows // 2
@@ -151,7 +159,6 @@
 
     parts = sems.shape[0]
     step = out.shape[0] // parts
-    pairs_copy.wait()
     copies = []
     for i in range(parts):
         span = slice(i * step, (i + 1) * step)
@@ -169,30 +176,28 @@
         copy.wait()
 
 
-def products_of(turned, places, tile_pairs, frames_all):
+def products_of(turned, places, pairs, frames_all):
     sources, rows, width = turned.shape
-    npairs = tile_pairs.shape[0]
+    npairs = pairs.shape[1]
     depth = len(places[0]) * rows
     tiles = len(places) * width // TILE
     return pl.pallas_call(
         functools.partial(pairs_kernel, 1.0 / frames_all, places),
         out_shape=jax.ShapeDtypeStruct((npairs, TILE, 2 * TILE), jnp.bfloat16),
         in_specs=[
-            pl.BlockSpec(memory_space=pl.ANY),
+            pl.BlockSpec(memory_space=pltpu.SMEM),
             pl.BlockSpec(memory_space=pltpu.VMEM),
         ],
         out_specs=pl.BlockSpec(memory_space=pl.ANY),
         scratch_shapes=[
-            pltpu.SMEM((2, npairs), jnp.int32),
             pltpu.VMEM((tiles, TILE, depth), jnp.bfloat16),
             pltpu.VMEM((tiles, depth, 2 * TILE), jnp.bfloat16),
             pltpu.VMEM((npairs, TILE, 2 * TILE), jnp.bfloat16),
-            pltpu.SemaphoreType.DMA,
             pltpu.SemaphoreType.DMA((npairs // divisor(npairs, 32),)),
         ],
         compiler_params=pltpu.CompilerParams(vmem_limit_bytes=VMEM_LIMIT),
         name="pair_products",
-    )(tile_pairs.T, turned)
+    )(pairs, turned)
 
 
 def turn_group(n_wide, n_time):
@@ -216,7 +221,7 @@
     place = {d: j for j, d in enumerate(group)}
     order = [d * per_dev + c for d in group for c in range(per_dev)]
 
-    spectra = spectra_of(voltages, channels, order)
+    spectra, pairs = spectra_of(voltages, channels, tile_pairs, order)
     turned = lax.all_to_all(
         spectra, ("wide", "tm"), split_axis=0, concat_axis=0, axis_index_groups=[group], tiled=True
     )
@@ -230,7 +235,7 @@
             one = one.reshape(n_wide, n_time, rows, in_dev).transpose(1, 2, 0, 3)
             one = one.reshape(n_time, rows, n_wide * in_dev)
             places = [list(range(n_time))]
-        results.append(products_of(one, places, tile_pairs, frames_dev * n_time))
+        results.append(products_of(one, places, pairs, frames_dev * n_time))
     return jnp.stack(results)
 
 

time: 18.2 us -> 17.8 us (0.978)
  Pallas kernels: 6.75 us -> 6.44 us
    pallas_call x1, Pallas kernels: 2.18 us -> 1.9 us  [products_of(): pl.pallas_call(functools.partial(pairs_kernel, 1.0 / frames_all, places),...]
where the time goes in v6:
time: 17.8 us; the launch traced here: 17.6 us
  blocking collectives  11.1 us (62%)
  Pallas kernels  6.44 us (36%)
    all_to_all x1, blocking collectives, shards(): lax.all_to_all(spectra, ('wide', 'tm'), split_axis=0, concat_axis=0, axis...  11.1 us
    pallas_call x1, Pallas kernels, spectra_of(): pl.pallas_call(functools.partial(spectra_kernel, order), out_shape=(jax.S...  4.54 us
    pallas_call x1, Pallas kernels, products_of(): pl.pallas_call(functools.partial(pairs_kernel, 1.0 / frames_all, places),...  1.9 us

profile of v6, /device:TPU:0, one launch (start us, length us, event | category | flops | bytes accessed | tf_op | source)
XLA Modules:
  0.0 17.6 jit_solution(9224099097633011479)
XLA Ops:
  0.0 4.5 %spectra.1 = (bf16[16,16,256]{2,1,0:T(8,128)(2,1)S(1)}, s32[2,128]{1,0:T(2,128)S(4)}) custom-call(s32[16]{0:T(128)} %chan_hbm.1, s32[2,128]{1,0:T(2,128)} %bitcast.2, bf16[256,16384]{1,0:T(8,128)(2,1)} %volt_hbm.1), custom_call_target="tpu_custom_call" | custom-call | tf_op jit(solution)/shard_map/spectra/pallas_call | solution.py:109
  4.5 11.1 %all_to_all.5.turned_ref = bf16[16,16,256]{2,1,0:T(8,128)(2,1)S(1)} all-to-all(bf16[16,16,256]{2,1,0:T(8,128)(2,1)S(1)} %get-tuple-element.8), channel_id=1, replica_groups={{11,0,1,2,3,4,5,6,7,12,13,14,15,8,9,10},{27,16,17,18,19,20,21,22,23,28,..., dimensions={0} | all-to-all | bytes 262144 | tf_op jit(solution)/shard_map/all_to_all | solution.py:225
  15.7 1.9 %pair_products.1 = bf16[128,64,128]{2,1,0:T(8,128)(2,1)} custom-call(s32[2,128]{1,0:T(2,128)S(4)} %get-tuple-element.7.pairs_ref, bf16[16,16,256]{2,1,0:T(8,128)(2,1)S(1)} %all_to_all.5.turned_ref), custom_call_target="tpu_custom_call" | custom-call | tf_op jit(solution)/shard_map/pair_products/pallas_call | solution.py:184

commit v7 on v6

--- a/solution.py
+++ b/solution.py
@@ -1,5 +1,6 @@
 import functools
 import math
+import random
 
 import jax
 import jax.numpy as jnp
@@ -202,9 +203,9 @@
 
 def turn_group(n_wide, n_time):
     middle = (n_wide // 2 + 1) * n_time - 1 + (n_time if n_wide > 2 else 0)
-    plane = 2 * n_time
     others = [d for d in range(n_wide * n_time) if d != middle]
-    return [middle] + sorted(others, key=lambda d: (-abs(d // plane - middle // plane), d))
+    random.Random(10).shuffle(others)
+    return [middle] + others
 
 
 def shards(voltages, channels, tile_pairs):

time: 17.8 us -> 17.5 us (0.983)
  blocking collectives: 11.1 us -> 10.9 us
    all_to_all x1, blocking collectives: 11.1 us -> 10.9 us  [shards(): lax.all_to_all(spectra, ('wide', 'tm'), split_axis=0, concat_axis=0, axis...]
where the time goes in v7:
time: 17.5 us; the launch traced here: 17.3 us
  blocking collectives  10.9 us (62%)
  Pallas kernels  6.44 us (37%)
    all_to_all x1, blocking collectives, shards(): lax.all_to_all(spectra, ('wide', 'tm'), split_axis=0, concat_axis=0, axis...  10.9 us
    pallas_call x1, Pallas kernels, spectra_of(): pl.pallas_call(functools.partial(spectra_kernel, order), out_shape=(jax.S...  4.54 us
    pallas_call x1, Pallas kernels, products_of(): pl.pallas_call(functools.partial(pairs_kernel, 1.0 / frames_all, places),...  1.9 us

profile of v7, /device:TPU:0, one launch (start us, length us, event | category | flops | bytes accessed | tf_op | source)
XLA Modules:
  0.0 17.3 jit_solution(3041099169642450066)
XLA Ops:
  0.0 4.5 %spectra.1 = (bf16[16,16,256]{2,1,0:T(8,128)(2,1)S(1)}, s32[2,128]{1,0:T(2,128)S(4)}) custom-call(s32[16]{0:T(128)} %chan_hbm.1, s32[2,128]{1,0:T(2,128)} %bitcast.2, bf16[256,16384]{1,0:T(8,128)(2,1)} %volt_hbm.1), custom_call_target="tpu_custom_call" | custom-call | tf_op jit(solution)/shard_map/spectra/pallas_call | solution.py:110
  4.5 10.9 %all_to_all.5.turned_ref = bf16[16,16,256]{2,1,0:T(8,128)(2,1)S(1)} all-to-all(bf16[16,16,256]{2,1,0:T(8,128)(2,1)S(1)} %get-tuple-element.8), channel_id=1, replica_groups={{11,4,5,10,1,2,8,13,12,3,14,15,7,6,0,9},{27,20,21,26,17,18,24,29,28,19,..., dimensions={0} | all-to-all | bytes 262144 | tf_op jit(solution)/shard_map/all_to_all | solution.py:226
  15.4 1.9 %pair_products.1 = bf16[128,64,128]{2,1,0:T(8,128)(2,1)} custom-call(s32[2,128]{1,0:T(2,128)S(4)} %get-tuple-element.7.pairs_ref, bf16[16,16,256]{2,1,0:T(8,128)(2,1)S(1)} %all_to_all.5.turned_ref), custom_call_target="tpu_custom_call" | custom-call | tf_op jit(solution)/shard_map/pair_products/pallas_call | solution.py:185

commit v8 on v7

--- a/solution.py
+++ b/solution.py
@@ -67,14 +67,13 @@
     chan_copy = pltpu.make_async_copy(chan_hbm, chan, list_sems.at[0])
     chan_copy.start()
     pairs_copy = pltpu.make_async_copy(pairs_hbm, pairs_ref, list_sems.at[1])
-    pairs_copy.start()
 
     @pl.loop(0, frames)
     def _(f):
         frame(f).start()
 
+    pairs_copy.start()
     chan_copy.wait()
-    pairs_copy.wait()
     fill_table(order, chan, table)
 
     def transform(f, several):
@@ -100,6 +99,7 @@
         transform(singles + 2 * g, 2)
 
     out_ref[...] = spec[...].astype(out_ref.dtype)
+    pairs_copy.wait()
 
 
 def spectra_of(voltages, channels, tile_pairs, order):
@@ -140,7 +140,7 @@
         stack = []
         for t in range(times):
             x = turned_ref[place[t]].astype(jnp.float32)
-            stack.append(x)
+            stack.append(turned_ref[place[t]])
             m = jnp.concatenate([x[half:], -x[:half]], 0)
             for u in range(width // LANES):
                 xu = x[:, u * LANES : (u + 1) * LANES]
@@ -153,7 +153,7 @@
                 right[tile + 1, depth] = second.astype(right.dtype)
         stack = jnp.concatenate(stack, 0)
         for u in range(width // LANES):
-            turned = stack[:, u * LANES : (u + 1) * LANES].T.astype(left.dtype)
+            turned = stack[:, u * LANES : (u + 1) * LANES].T
             tile = (w * width + u * LANES) // TILE
             left[tile] = turned[:TILE]
             left[tile + 1] = turned[TILE:]
@@ -194,7 +194,7 @@
             pltpu.VMEM((tiles, TILE, depth), jnp.bfloat16),
             pltpu.VMEM((tiles, depth, 2 * TILE), jnp.bfloat16),
             pltpu.VMEM((npairs, TILE, 2 * TILE), jnp.bfloat16),
-            pltpu.SemaphoreType.DMA((npairs // divisor(npairs, 32),)),
+            pltpu.SemaphoreType.DMA((npairs // divisor(npairs, 16),)),
         ],
         compiler_params=pltpu.CompilerParams(vmem_limit_bytes=VMEM_LIMIT),
         name="pair_products",

time: 17.5 us -> 17.5 us (level)
  no operation moved by 1% of the time
where the time goes in v8:
time: 17.5 us; the launch traced here: 17.3 us
  blocking collectives  10.9 us (62%)
  Pallas kernels  6.4 us (37%)
    all_to_all x1, blocking collectives, shards(): lax.all_to_all(spectra, ('wide', 'tm'), split_axis=0, concat_axis=0, axis...  10.9 us
    pallas_call x1, Pallas kernels, spectra_of(): pl.pallas_call(functools.partial(spectra_kernel, order), out_shape=(jax.S...  4.55 us
    pallas_call x1, Pallas kernels, products_of(): pl.pallas_call(functools.partial(pairs_kernel, 1.0 / frames_all, places),...  1.85 us

profile of v8, /device:TPU:0, one launch (start us, length us, event | category | flops | bytes accessed | tf_op | source)
XLA Modules:
  0.0 17.3 jit_solution(13271336676259083558)
XLA Ops:
  0.0 4.5 %spectra.1 = (bf16[16,16,256]{2,1,0:T(8,128)(2,1)S(1)}, s32[2,128]{1,0:T(2,128)S(4)}) custom-call(s32[16]{0:T(128)} %chan_hbm.1, s32[2,128]{1,0:T(2,128)} %bitcast.2, bf16[256,16384]{1,0:T(8,128)(2,1)} %volt_hbm.1), custom_call_target="tpu_custom_call" | custom-call | tf_op jit(solution)/shard_map/spectra/pallas_call | solution.py:110
  4.6 10.9 %all_to_all.5.turned_ref = bf16[16,16,256]{2,1,0:T(8,128)(2,1)S(1)} all-to-all(bf16[16,16,256]{2,1,0:T(8,128)(2,1)S(1)} %get-tuple-element.8), channel_id=1, replica_groups={{11,4,5,10,1,2,8,13,12,3,14,15,7,6,0,9},{27,20,21,26,17,18,24,29,28,19,..., dimensions={0} | all-to-all | bytes 262144 | tf_op jit(solution)/shard_map/all_to_all | solution.py:226
  15.4 1.8 %pair_products.1 = bf16[128,64,128]{2,1,0:T(8,128)(2,1)} custom-call(s32[2,128]{1,0:T(2,128)S(4)} %get-tuple-element.7.pairs_ref, bf16[16,16,256]{2,1,0:T(8,128)(2,1)S(1)} %all_to_all.5.turned_ref), custom_call_target="tpu_custom_call" | custom-call | tf_op jit(solution)/shard_map/pair_products/pallas_call | solution.py:185

commit v9 on v8

--- a/solution.py
+++ b/solution.py
@@ -79,12 +79,16 @@
     def transform(f, several):
         for k in range(several):
             frame(f + k).wait()
-        block = volt[pl.ds(f, several)].reshape(several * in_dev, NFFT)
-        result = lax.dot_general(
-            table[...], block, (((1,), (1,)), ((), ())), preferred_element_type=jnp.float32
-        )
-        for k in range(several):
-            part = result[:, k * in_dev : (k + 1) * in_dev]
+        results = [
+            lax.dot_general(
+                table[...],
+                volt[f + k],
+                (((1,), (1,)), ((), ())),
+                preferred_element_type=jnp.float32,
+            )
+            for k in range(several)
+        ]
+        for k, part in enumerate(results):
             spec[:, pl.ds(f + k, 1), :] = part[:count].reshape(count, 1, in_dev)
             spec[:, pl.ds(frames + f + k, 1), :] = part[count:].reshape(count, 1, in_dev)
 

time: 17.5 us -> 17.5 us (level)
  no operation moved by 1% of the time
where the time goes in v9:
time: 17.5 us; the launch traced here: 17.3 us
  blocking collectives  10.9 us (62%)
  Pallas kernels  6.39 us (37%)
    all_to_all x1, blocking collectives, shards(): lax.all_to_all(spectra, ('wide', 'tm'), split_axis=0, concat_axis=0, axis...  10.9 us
    pallas_call x1, Pallas kernels, spectra_of(): pl.pallas_call(functools.partial(spectra_kernel, order), out_shape=(jax.S...  4.54 us
    pallas_call x1, Pallas kernels, products_of(): pl.pallas_call(functools.partial(pairs_kernel, 1.0 / frames_all, places),...  1.85 us

profile of v9, /device:TPU:0, one launch (start us, length us, event | category | flops | bytes accessed | tf_op | source)
XLA Modules:
  0.0 17.3 jit_solution(15038838057778974451)
XLA Ops:
  0.0 4.5 %spectra.1 = (bf16[16,16,256]{2,1,0:T(8,128)(2,1)S(1)}, s32[2,128]{1,0:T(2,128)S(4)}) custom-call(s32[16]{0:T(128)} %chan_hbm.1, s32[2,128]{1,0:T(2,128)} %bitcast.2, bf16[256,16384]{1,0:T(8,128)(2,1)} %volt_hbm.1), custom_call_target="tpu_custom_call" | custom-call | tf_op jit(solution)/shard_map/spectra/pallas_call | solution.py:114
  4.6 10.9 %all_to_all.5.turned_ref = bf16[16,16,256]{2,1,0:T(8,128)(2,1)S(1)} all-to-all(bf16[16,16,256]{2,1,0:T(8,128)(2,1)S(1)} %get-tuple-element.8), channel_id=1, replica_groups={{11,4,5,10,1,2,8,13,12,3,14,15,7,6,0,9},{27,20,21,26,17,18,24,29,28,19,..., dimensions={0} | all-to-all | bytes 262144 | tf_op jit(solution)/shard_map/all_to_all | solution.py:230
  15.4 1.8 %pair_products.1 = bf16[128,64,128]{2,1,0:T(8,128)(2,1)} custom-call(s32[2,128]{1,0:T(2,128)S(4)} %get-tuple-element.7.pairs_ref, bf16[16,16,256]{2,1,0:T(8,128)(2,1)S(1)} %all_to_all.5.turned_ref), custom_call_target="tpu_custom_call" | custom-call | tf_op jit(solution)/shard_map/pair_products/pallas_call | solution.py:189
